TPU v7x, 32 devices: a whole 2x2x4 slice. The times are simulated.
32 devices in a mesh: seq: 16 (over z, y, x), tp: 2 (over core).
Axes of the slice: x: 2, y: 2, z: 4, core: 2. Of those that a mesh axis runs over, the one named last changes fastest.
Arguments:
- queries: bfloat16 [16, 4, 8192], P('seq', None, 'tp'), may hold values from -40 to 40
- new_keys: bfloat16 [16, 4, 1024], P('seq', None, 'tp'), may hold values from -6 to 6
- new_values: bfloat16 [16, 4, 1024], P('seq', None, 'tp'), may hold values from -6 to 6
- prefix_keys: bfloat16 [8, 3072, 1024], P(None, 'seq', 'tp'), may hold values from -8 to 8
- prefix_values: bfloat16 [8, 3072, 1024], P(None, 'seq', 'tp'), may hold values from -6 to 6
- page_keys: bfloat16 [256, 64, 1024], P('seq', None, 'tp'), may hold values from -6 to 6
- page_values: bfloat16 [256, 64, 1024], P('seq', None, 'tp'), may hold values from -6 to 6
- out_weight: bfloat16 [8192, 8192], P('tp', 'seq'), may hold values from -0.5 to 0.5
- group_of: int32 [16], replicated, may hold values from 0 to 7, as said below
- prefix_len: int32 [8], replicated, may hold values from 2 to 3072, as said below
- total_len: int32 [16], replicated, may hold values from 3 to 7168, as said below
- page_owner: int32 [256], P('seq'), may hold values from 0 to 15, as said below
- page_slot: int32 [256], P('seq'), may hold values from 0 to 63, as said below
- new_valid: int32 [16, 4], replicated, may hold values from 0 to 1, as said below
Outputs:
- attn_out: bfloat16 [64, 8192], P('tp', 'seq')
Inputs may be any that keep to these rules, and one draw needn't show every extreme that they name: `group_of`: every one of the 8 groups has at least one request. `prefix_len`: some group's prefix holds exactly 3072 tokens. `page_owner`: every request owns at least one page and at most 64 pages; one request owns exactly 64. `page_slot`: the pages of one request carry the slots 0, 1, 2 and so on, each once. A request's pages are full except the one of its highest slot, which holds 1 to 64 tokens; total_len is its group's prefix length plus these tokens. `new_valid`: each row is a run of ones followed by zeros, and its first entry is one.
All inputs are finite; a program needn't handle non-finite values.
Results may differ from a plain program's by a relative error of at most 0.022.
Values may be sent and summed in bfloat16 or wider, within the bound.
A program may use at most 192 MiB of HBM per device.

v0:
```python
import jax
import jax.numpy as jnp
from jax import lax
from jax.sharding import PartitionSpec as P

HEAD_DIM = 128
HPK = 8
GROUPS = 8
NEW = 4


NEG = -1e30


def merged(part, axis, combine):
    gathered = jax.tree.map(lambda a: lax.all_gather(a, axis), part)

    def take(source):
        return jax.tree.map(lambda a: lax.dynamic_index_in_dim(a, source, 0, False), gathered)

    return lax.fori_loop(
        1, lax.axis_size(axis), lambda source, state: combine(state, take(source)), take(0)
    )


def softmax_part(scores, key_mask):
    masked = jnp.where(key_mask, scores, NEG)
    row_peak = jnp.max(masked, axis=-1)
    weights = jnp.where(key_mask, jnp.exp(masked - row_peak[..., None]), 0.0)
    return (row_peak, jnp.sum(weights, axis=-1), weights.astype(jnp.bfloat16))


def combine(first_part, second_part):
    peak_a, total_a, out_a = first_part
    peak_b, total_b, out_b = second_part
    top_peak = jnp.maximum(peak_a, peak_b)
    factor_a = jnp.exp(peak_a - top_peak)
    factor_b = jnp.exp(peak_b - top_peak)
    return (
        top_peak,
        total_a * factor_a + total_b * factor_b,
        out_a * factor_a[..., None] + out_b * factor_b[..., None],
    )


def local(
    queries,
    new_keys,
    new_values,
    prefix_keys,
    prefix_values,
    page_keys,
    page_values,
    out_weight,
    group_of,
    prefix_len,
    total_len,
    page_owner,
    page_slot,
    new_valid,
):
    req_dev = queries.shape[0]
    seq_count = lax.axis_size("seq")
    requests = req_dev * seq_count
    kv_local = new_keys.shape[2] // HEAD_DIM
    heads_local = kv_local * HPK
    score_scale = HEAD_DIM ** (-0.5)
    seq_idx = lax.axis_index("seq")
    gathered = lax.all_gather(queries, "seq", axis=0, tiled=True)
    query_all = gathered.reshape(requests, NEW, kv_local, HPK, HEAD_DIM)
    group_hot = group_of[:, None] == jnp.arange(GROUPS, dtype=jnp.int32)[None, :]
    own_prefix = jnp.sum(jnp.where(group_hot, prefix_len[None, :], 0), axis=1)
    suffix_len = total_len - own_prefix
    pre_dev = prefix_keys.shape[1]
    positions = seq_idx * pre_dev + jnp.arange(pre_dev, dtype=jnp.int32)
    pre_keys = prefix_keys.reshape(GROUPS, pre_dev, kv_local, HEAD_DIM)
    pre_values = prefix_values.reshape(GROUPS, pre_dev, kv_local, HEAD_DIM)
    partial_value = (
        jnp.full((requests, NEW, kv_local, HPK), NEG, jnp.float32),
        jnp.zeros((requests, NEW, kv_local, HPK), jnp.float32),
        jnp.zeros((requests, NEW, kv_local, HPK, HEAD_DIM), jnp.float32),
    )
    for group_idx in range(GROUPS):
        scores = (
            jnp.einsum(
                "rjkhd,ikd->rjkhi",
                query_all,
                pre_keys[group_idx],
                preferred_element_type=jnp.float32,
            )
            * score_scale
        )
        member = group_hot[:, group_idx]
        live_keys = positions < prefix_len[group_idx]
        key_mask = member[:, None, None, None, None] & live_keys[None, None, None, None, :]
        row_peak, row_total, weights = softmax_part(scores, key_mask)
        values = jnp.einsum(
            "rjkhi,ikd->rjkhd", weights, pre_values[group_idx], preferred_element_type=jnp.float32
        )
        chosen = member[:, None, None, None]
        partial_value = (
            jnp.where(chosen, row_peak, partial_value[0]),
            jnp.where(chosen, row_total, partial_value[1]),
            jnp.where(chosen[..., None], values, partial_value[2]),
        )
    prefix_part = partial_value
    page_count = page_keys.shape[0]
    page_len = page_keys.shape[1]
    key_pages = page_keys.reshape(page_count, page_len, kv_local, HEAD_DIM)
    value_pages = page_values.reshape(page_count, page_len, kv_local, HEAD_DIM)
    owner_hot = page_owner[:, None] == jnp.arange(requests, dtype=jnp.int32)[None, :]
    own_suffix = jnp.sum(jnp.where(owner_hot, suffix_len[None, :], 0), axis=1)
    page_queries = jnp.take(query_all, page_owner, axis=0)
    scores = (
        jnp.einsum("pjkhd,pikd->pjkhi", page_queries, key_pages, preferred_element_type=jnp.float32)
        * score_scale
    )
    offsets = page_slot[:, None] * page_len + jnp.arange(page_len, dtype=jnp.int32)[None, :]
    live_keys = offsets < own_suffix[:, None]
    page_peak, page_total, weights = softmax_part(scores, live_keys[:, None, None, None, :])
    page_out = jnp.einsum(
        "pjkhi,pikd->pjkhd", weights, value_pages, preferred_element_type=jnp.float32
    )
    owner_wide = owner_hot[:, :, None, None, None]
    device_peak = jnp.max(jnp.where(owner_wide, page_peak[:, None], NEG), axis=0)
    page_back = jnp.max(jnp.where(owner_wide, device_peak[None], NEG), axis=1)
    factor = jnp.exp(page_peak - page_back)
    owner_float = owner_hot.astype(jnp.float32)
    suffix_total = jnp.einsum(
        "pr,pjkh->rjkh", owner_float, page_total * factor, precision=lax.Precision.HIGHEST
    )
    suffix_out = jnp.einsum(
        "pr,pjkhd->rjkhd",
        owner_float,
        page_out * factor[..., None],
        precision=lax.Precision.HIGHEST,
    )
    partial_value = combine(prefix_part, (device_peak, suffix_total, suffix_out))
    row_start = seq_idx * req_dev
    local_queries = queries.reshape(req_dev, NEW, kv_local, HPK, HEAD_DIM)
    local_keys = new_keys.reshape(req_dev, NEW, kv_local, HEAD_DIM)
    local_values = new_values.reshape(req_dev, NEW, kv_local, HEAD_DIM)
    valid_local = lax.dynamic_slice_in_dim(new_valid, row_start, req_dev, 0)
    scores = (
        jnp.einsum(
            "rjkhd,rikd->rjkhi", local_queries, local_keys, preferred_element_type=jnp.float32
        )
        * score_scale
    )
    causal = jnp.arange(NEW, dtype=jnp.int32)[None, :] <= jnp.arange(NEW, dtype=jnp.int32)[:, None]
    key_mask = causal[None, :, None, None, :] & (valid_local[:, None, None, None, :] == 1)
    row_peak, row_total, weights = softmax_part(scores, key_mask)
    new_out = jnp.einsum(
        "rjkhi,rikd->rjkhd", weights, local_values, preferred_element_type=jnp.float32
    )
    own_rows = (
        lax.dynamic_slice_in_dim(partial_value[0], row_start, req_dev, 0),
        lax.dynamic_slice_in_dim(partial_value[1], row_start, req_dev, 0),
        lax.dynamic_slice_in_dim(partial_value[2], row_start, req_dev, 0),
    )
    own_part = combine(own_rows, (row_peak, row_total, new_out))
    partial_value = (
        lax.dynamic_update_slice_in_dim(partial_value[0], own_part[0], row_start, 0),
        lax.dynamic_update_slice_in_dim(partial_value[1], own_part[1], row_start, 0),
        lax.dynamic_update_slice_in_dim(partial_value[2], own_part[2], row_start, 0),
    )
    final_peak, final_total, final_out = merged(partial_value, "seq", combine)
    valid_rows = new_valid.astype(jnp.float32)[:, :, None, None, None]
    attention = (final_out / final_total[..., None] * valid_rows).astype(jnp.bfloat16)
    attention = attention.reshape(requests * NEW, heads_local * HEAD_DIM)
    terms = jnp.dot(attention, out_weight, preferred_element_type=jnp.float32)
    summed = lax.psum_scatter(terms.astype(jnp.bfloat16), "tp", scatter_dimension=0, tiled=True)
    return summed


def solution(mesh):
    placed = (
        P("seq", None, "tp"),
        P("seq", None, "tp"),
        P("seq", None, "tp"),
        P(None, "seq", "tp"),
        P(None, "seq", "tp"),
        P("seq", None, "tp"),
        P("seq", None, "tp"),
        P("tp", "seq"),
        P(),
        P(),
        P(),
        P("seq"),
        P("seq"),
        P(),
    )
    return jax.shard_map(
        local, mesh=mesh, in_specs=placed, out_specs=P("tp", "seq"), check_vma=False
    )
```

profile of v0, /device:TPU:1, one launch (start us, length us, event | category | flops | bytes accessed | tf_op | source)
XLA Modules:
  0.0 422.9 jit_solution(11418753738771807706)
XLA Ops:
  11.6 38.0 %all_gather.25 = bf16[16,4,4096]{2,1,0:T(4,128)(2,1)S(1)} all-gather(bf16[1,4,4096]{2,1,0:T(4,128)(2,1)} %param.16), channel_id=1, replica_groups=mesh['seq'=16,'tp'=2] {'seq'}, dimensions={0}, use_global_device_ids=true | all-gather | bytes 557056 | tf_op jit(solution)/shard_map/all_gather | solution.py:69
  52.9 2.3 fusion.131
  65.2 1.8 squeeze.118
  73.2 2.0 fusion.52
  86.1 1.7 squeeze.136
  90.8 2.1 reshape.614
  93.1 2.0 fusion.32
  95.1 2.2 fusion.41
  113.7 1.7 fusion.19
  117.1 1.8 fusion.23
  126.3 1.9 convolution_select_fusion
  139.5 47.0 %all_gather.27 = f32[16,16,4,4,8]{1,4,3,2,0:T(8,128)S(1)} all-gather(f32[1,16,4,4,8]{1,4,3,2,0:T(8,128)S(1)} %copy.342), channel_id=1, replica_groups=mesh['seq'=16,'tp'=2] {'seq'}, dimensions={0}, use_global_device_ids=true | all-gather | bytes 139264 | tf_op jit(solution)/shard_map/all_gather | solution.py:16
  186.5 50.2 %all_gather.30 = f32[16,16,4,4,8]{1,4,3,2,0:T(8,128)} all-gather(f32[1,16,4,4,8]{1,4,3,2,0:T(8,128)S(1)} %dynamic_update_slice.13), channel_id=1, replica_groups=mesh['seq'=16,'tp'=2] {'seq'}, dimensions={0}, use_global_device_ids=true | all-gather | bytes 139264 | tf_op jit(solution)/shard_map/all_gather | solution.py:16
  237.6 119.5 %all-gather.2.cloned.1.call-done = f32[16,16,4,4,8,128]{5,4,3,2,1,0:T(8,128)} async-done(((f32[1,16,4,4,8,128]{5,4,3,2,1,0:T(8,128)}), f32[16,16,4,4,8,128]{5,4,3,2,1,0:T(8,128)}) %all-gather.2.cloned.1.call-update) | async-done | bytes 16777232 | tf_op jit(solution)/shard_map/all_gather | solution.py:16
  358.4 46.6 %while.19 = (s32[]{:T(128)}, f32[16,4,4,8]{0,3,2,1:T(8,128)S(1)}, f32[16,4,4,8]{0,3,2,1:T(8,128)S(1)}, f32[16,4,4,8,128]{4,3,2,1,0:T(8,128)S(1)}, f32[16,16,4,4,...) while((s32[]{:T(128)}, f32[16,4,4,8]{0,3,2,1:T(8,128)S(1)}, ...), condition=%wide.region_25.26_spmd, body=%wide.region_24.25_spmd.sunk | while | flops 798725 | bytes 3260567 | solution.py:21
  359.6 1.9 fusion.139
  362.8 1.9 fusion.139
  365.9 1.9 fusion.139
  369.0 1.9 fusion.139
  372.1 1.9 fusion.139
  375.2 1.9 fusion.139
  378.3 1.9 fusion.139
  381.4 1.9 fusion.139
  384.5 1.9 fusion.139
  387.6 1.9 fusion.139
  390.7 1.9 fusion.139
  393.8 1.9 fusion.139
  396.9 1.9 fusion.139
  400.0 1.9 fusion.139
  403.2 1.9 fusion.139
  405.9 3.7 convolution_convert_fusion
  409.5 6.5 %reduce-scatter.2.cloned.1.call-done = bf16[32,512]{1,0:T(8,128)(2,1)} async-done(((bf16[64,512]{1,0:T(8,128)(2,1)}), bf16[32,512]{1,0:T(8,128)(2,1)}) %reduce-scatter.2.cloned.1.call-update) | async-done | bytes 32784 | tf_op jit(solution)/shard_map/reduce_scatter | solution.py:172
  (296 shorter events, 95.0 us)
Async XLA Ops:
  6.5 130.0 %copy-start = (bf16[1,4,512]{2,1,0:T(4,128)(2,1)S(1)}, bf16[1,4,512]{2,1,0:T(4,128)(2,1)}, u32[]{:S(2)}) copy-start(bf16[1,4,512]{2,1,0:T(4,128)(2,1)} %param.18) | copy-start | bytes 12292
  6.5 44.8 %copy-start.66 = (s32[16]{0:T(128)S(1)}, s32[16]{0:T(128)}, u32[]{:S(2)}) copy-start(s32[16]{0:T(128)} %param.27) | copy-start | bytes 196
  6.5 43.6 %copy-start.15 = (bf16[16,64,512]{2,1,0:T(8,128)(2,1)S(1)}, bf16[16,64,512]{2,1,0:T(8,128)(2,1)}, u32[]{:S(2)}) copy-start(bf16[16,64,512]{2,1,0:T(8,128)(2,1)} %param.21) | copy-start | bytes 3145732
  6.5 44.8 %copy-start.70 = (s32[16]{0:T(128)S(1)}, s32[16]{0:T(128)}, u32[]{:S(2)}) copy-start(s32[16]{0:T(128)} %param.26) | copy-start | bytes 196
  6.5 44.9 %copy-start.71 = (s32[16]{0:T(128)S(1)}, s32[16]{0:T(128)}, u32[]{:S(2)}) copy-start(s32[16]{0:T(128)} %param.28) | copy-start | bytes 196
  6.5 350.6 %all-gather.2.cloned.1.call-start = ((), (), s32[]{:S(2)}) async-start(), calls=%async_computation.1 | async-start | bytes 17825792 | tf_op jit(solution)/shard_map/all_gather | solution.py:16
  51.5 3.8 copy-start.62
  52.9 4.5 %copy-start.4 = (bf16[8,192,512]{2,1,0:T(8,128)(2,1)S(1)}, bf16[8,192,512]{2,1,0:T(8,128)(2,1)}, u32[]{:S(2)}) copy-start(bf16[8,192,512]{2,1,0:T(8,128)(2,1)} %param.19) | copy-start | bytes 4718596
  55.3 17.9 %copy-start.13 = (f32[16,4,4,8,64]{4,3,1,2,0:T(8,128)}, f32[16,4,4,8,64]{4,3,1,2,0:T(8,128)S(1)}, u32[]{:S(2)}) copy-start(f32[16,4,4,8,64]{4,3,1,2,0:T(8,128)S(1)} %get-tuple-element.291) | copy-start | bytes 1572868
  58.5 11.9 %copy-start.64 = (s32[16,4]{0,1:T(4,128)S(1)}, s32[16,4]{0,1:T(4,128)}, u32[]{:S(2)}) copy-start(s32[16,4]{0,1:T(4,128)} %param.29) | copy-start | bytes 772
  65.2 16.6 %copy-start.5 = (bf16[8,192,512]{2,1,0:T(8,128)(2,1)S(1)}, bf16[8,192,512]{2,1,0:T(8,128)(2,1)}, u32[]{:S(2)}) copy-start(bf16[8,192,512]{2,1,0:T(8,128)(2,1)} %param.20) | copy-start | bytes 4718596
  70.6 5.6 %copy-start.68 = (pred[4,4]{1,0:T(4,128)(4,1)}, pred[4,4]{1,0:T(4,128)(4,1)S(1)}, u32[]{:S(2)}) copy-start(pred[4,4]{1,0:T(4,128)(4,1)S(1)} %fusion.114) | copy-start | bytes 52
  71.6 4.6 %copy-start.39 = (f32[1,4,4,8,4]{3,4,1,2,0:T(4,128)}, f32[1,4,4,8,4]{3,4,1,2,0:T(4,128)S(1)}, u32[]{:S(2)}) copy-start(f32[1,4,4,8,4]{3,4,1,2,0:T(4,128)S(1)} %get-tuple-element.293) | copy-start | bytes 6148
  86.1 6.9 %copy-start.14 = (f32[16,4,4,8,64]{4,3,1,2,0:T(8,128)S(1)}, f32[16,4,4,8,64]{4,3,1,2,0:T(8,128)}, u32[]{:S(2)}) copy-start(f32[16,4,4,8,64]{4,3,1,2,0:T(8,128)} %copy-done.13) | copy-start | bytes 1572868
  86.1 6.9 %copy-start.63 = (pred[16,64]{1,0:T(8,128)(4,1)S(1)}, pred[16,64]{1,0:T(8,128)(4,1)}, u32[]{:S(2)}) copy-start(pred[16,64]{1,0:T(8,128)(4,1)} %copy-done.62) | copy-start | bytes 3076
  95.1 3.6 copy-start.60
  95.1 3.7 copy-start.30
  95.1 4.4 %copy-start.41 = (pred[16]{0:T(512)(128)(4,1)S(1)}, pred[16]{0:T(512)(128)(4,1)}, u32[]{:S(2)}) copy-start(pred[16]{0:T(512)(128)(4,1)} %get-tuple-element.260) | copy-start | bytes 52
  106.2 14.4 %copy-start.6 = (f32[16,4,4,8]{0,3,1,2:T(8,128)}, f32[16,4,4,8]{0,3,1,2:T(8,128)S(1)}, u32[]{:S(2)}) copy-start(f32[16,4,4,8]{0,3,1,2:T(8,128)S(1)} %get-tuple-element.284) | copy-start | bytes 24580
  108.3 12.3 %copy-start.8 = (f32[16,4,4,8]{0,3,1,2:T(8,128)}, f32[16,4,4,8]{0,3,1,2:T(8,128)S(1)}, u32[]{:S(2)}) copy-start(f32[16,4,4,8]{0,3,1,2:T(8,128)S(1)} %get-tuple-element.286) | copy-start | bytes 24580
  109.1 11.4 %copy-start.10 = (f32[16,4,4,8]{0,3,1,2:T(8,128)}, f32[16,4,4,8]{0,3,1,2:T(8,128)S(1)}, u32[]{:S(2)}) copy-start(f32[16,4,4,8]{0,3,1,2:T(8,128)S(1)} %get-tuple-element.288) | copy-start | bytes 24580
  135.9 3.2 copy-start.7
  135.9 3.2 copy-start.9
  135.9 3.2 copy-start.11
  135.9 3.2 copy-start.44
  135.9 3.2 copy-start.47
  135.9 3.2 copy-start.50
  136.0 3.2 copy-start.53
  136.0 3.2 copy-start.56
  136.0 3.2 copy-start.59
  136.0 3.2 copy-start.61
  138.8 277.2 %reduce-scatter.2.cloned.1.call-start = ((), (), s32[]{:S(2)}) async-start(), calls=%async_computation.2 | async-start | bytes 98304 | tf_op jit(solution)/shard_map/reduce_scatter | solution.py:172
  (42 other events, 67.7 us)
Sparse Core Ops, SparseCore 0:
  138.9 218.1 all-gather.1
  409.7 6.3 reduce-scatter.1
where the time goes:
time: 426 us; the launch traced here: 423 us
  blocking collectives  135 us (32%)
  waiting for transfers between devices  126 us (30%)
  other arithmetic  69.1 us (16%)
  local copies, waits for them, and re-layouts  51.9 us (12%)
  matrix products  25.5 us (6%)
  between operations  14.4 us (3%)
    all_gather x1, waiting for transfers between devices, merged(): gathered = jax.tree.map(lambda a: lax.all_gather(a, axis), part)  119 us
    all_gather x2, blocking collectives, merged(): gathered = jax.tree.map(lambda a: lax.all_gather(a, axis), part)  97.2 us
    all_gather x1, blocking collectives, local(): gathered = lax.all_gather(queries, 'seq', axis=0, tiled=True)  38 us
    add x15, other arithmetic, combine(): out_a * factor_a[..., None] + out_b * factor_b[..., None]  28.4 us
    add x16, other arithmetic, combine(): total_a * factor_a + total_b * factor_b  14.5 us
    squeeze x8, local copies, waits for them, and re-layouts, local(): pre_keys[group_idx]  11.8 us
    convert_element_type x8, other arithmetic, softmax_part(): return (row_peak, jnp.sum(weights, axis=-1), weights.astype(jnp.bfloat16))  11.4 us
    squeeze x8, local copies, waits for them, and re-layouts, local(): pre_values[group_idx]  9.64 us
  transfers between devices with their start and end apart: 2, of which 2 were waited for; matrix products, arithmetic and copies ran while one was open for 0% of the time, Pallas kernels for 0%

commit v1 on v0

v1 whole, which is shorter than its diff:
```python
import functools
import math

import jax
import jax.numpy as jnp
from jax import lax
from jax.experimental import pallas as pl
from jax.experimental.pallas import tpu as pltpu
from jax.sharding import PartitionSpec as P

HEAD_DIM = 128
HPK = 8
GROUPS = 8
NEW = 4
ROWS = HPK * NEW
BLOCK_REQS = 16
CHUNK_REQS = 4
TILE = 128
NEG = -1e30
MESH = pl.DeviceIdType.MESH
F32 = jnp.float32
BF16 = jnp.bfloat16


def kernel(
    cfg,
    group_ref,
    plen_ref,
    tlen_ref,
    owner_ref,
    slot_ref,
    valid_ref,
    q_ref,
    nk_ref,
    nv_ref,
    pk_hbm,
    pv_hbm,
    gk_hbm,
    gv_hbm,
    w_hbm,
    out_ref,
    kall,
    vall,
    wall,
    vt,
    mask,
    tmp,
    qtmp,
    qbuf,
    s_scr,
    osend,
    ssend,
    obuf,
    sbuf,
    asend,
    abuf,
    tsend,
    tbuf,
    load_sem,
    q_send,
    q_recv,
    o_send,
    o_recv,
    s_send,
    s_recv,
    a_send,
    a_recv,
    t_send,
    t_recv,
):
    n, tp, reqs, kvs, pre, pages, page = cfg
    pre_rows, page_rows = GROUPS * pre, pages * page
    cached = pre_rows + page_rows
    keys = cached + TILE
    chunk = 384 if keys % 384 == 0 else TILE
    blocks = reqs // BLOCK_REQS
    brows = BLOCK_REQS * ROWS
    per_kv = reqs // CHUNK_REQS
    combiners = kvs * per_kv
    per_block = BLOCK_REQS // CHUNK_REQS
    me = lax.axis_index("seq")
    core = lax.axis_index("tp")
    all_combine = combiners == n

    loads = [
        pltpu.make_async_copy(src, dst, load_sem.at[i])
        for i, (src, dst) in enumerate(
            (
                (pv_hbm, vall.at[pl.ds(0, pre_rows)]),
                (gv_hbm, vall.at[pl.ds(pre_rows, page_rows)]),
                (pk_hbm, kall.at[pl.ds(0, pre_rows)]),
                (gk_hbm, kall.at[pl.ds(pre_rows, page_rows)]),
                (w_hbm, wall),
            )
        )
    ]
    for load in loads:
        load.start()

    barrier = pltpu.get_barrier_semaphore()

    def greet(k, c):
        pl.semaphore_signal(
            barrier, inc=1, device_id={"seq": lax.rem(me + k, n)}, device_id_type=MESH
        )
        return c

    lax.fori_loop(1, n, greet, 0)
    for k in range(1, tp):
        pl.semaphore_signal(
            barrier, inc=1, device_id={"tp": lax.rem(core + k, tp)}, device_id_type=MESH
        )

    q = q_ref[0].astype(F32)
    for h in range(kvs * HPK):
        qtmp[pl.ds(h * NEW, NEW), :] = q[:, h * HEAD_DIM : (h + 1) * HEAD_DIM]
    qbuf[me] = qtmp[...].reshape(kvs, ROWS, HEAD_DIM).astype(BF16)

    pl.semaphore_wait(barrier, n - 1 + tp - 1)

    def to_seq(src, dst, send, recv, peer):
        return pltpu.make_async_remote_copy(
            src_ref=src,
            dst_ref=dst,
            send_sem=send,
            recv_sem=recv,
            device_id={"seq": peer},
            device_id_type=MESH,
        )

    def q_copy(k, source):
        return to_seq(
            qbuf.at[source], qbuf.at[source], q_send.at[k], q_recv.at[source], lax.rem(me + k, n)
        )

    def q_start(k, c):
        q_copy(k, me).start()
        return c

    lax.fori_loop(1, n, q_start, 0)

    lane = lax.broadcasted_iota(jnp.int32, (1, TILE), 1)
    group_vec = jnp.full((1, TILE), -1, jnp.int32)
    total_vec = jnp.zeros((1, TILE), jnp.int32)
    for r in range(reqs):
        group_vec = jnp.where(lane == r, group_ref[r], group_vec)
        total_vec = jnp.where(lane == r, tlen_ref[r], total_vec)
    own_pre = jnp.zeros((1, TILE), jnp.int32)
    for g in range(GROUPS):
        own_pre = jnp.where(group_vec == g, plen_ref[g], own_pre)
    suffix_vec = total_vec - own_pre
    lane_pre = lax.broadcasted_iota(jnp.int32, (pre, TILE), 1)
    pos = me * pre + lax.broadcasted_iota(jnp.int32, (pre, TILE), 0)
    for g in range(GROUPS):
        limit = jnp.where(group_vec == g, plen_ref[g], 0)
        dead = (pos >= limit) & (lane_pre < reqs)
        mask[pl.ds(g * pre, pre), :] = jnp.where(dead, NEG, 0.0).astype(BF16)
    lane_page = lax.broadcasted_iota(jnp.int32, (page, TILE), 1)
    offset = lax.broadcasted_iota(jnp.int32, (page, TILE), 0)
    for p in range(pages):
        limit = jnp.where(lane == owner_ref[p], suffix_vec, 0)
        dead = (offset + slot_ref[p] * page >= limit) & (lane_page < reqs)
        mask[pl.ds(pre_rows + p * page, page), :] = jnp.where(dead, NEG, 0.0).astype(BF16)
    lane_new = lax.broadcasted_iota(jnp.int32, (TILE, TILE), 1)
    row_new = lax.broadcasted_iota(jnp.int32, (TILE, TILE), 0)
    valid_rows = jnp.zeros((TILE, TILE), jnp.int32)
    for i in range(NEW):
        valid_rows = jnp.where(row_new == i, valid_ref[me, i], valid_rows)
    alive = (
        (valid_rows == 1)
        & ((lane_new == me) | ((lane_new >= reqs) & (row_new <= lane_new - reqs)))
        & (row_new < NEW)
    )
    mask[pl.ds(cached, TILE), :] = jnp.where(alive, 0.0, NEG).astype(BF16)

    for new_ref, all_ref in ((nk_ref, kall), (nv_ref, vall)):
        tmp[...] = jnp.zeros_like(tmp)
        tmp[pl.ds(0, NEW), :] = new_ref[0].astype(F32)
        all_ref[pl.ds(cached, 16), :] = tmp[...].astype(BF16)
        all_ref[pl.ds(cached + 16, TILE - 16), :] = jnp.zeros((TILE - 16, kvs * HEAD_DIM), BF16)

    loads[0].wait()
    loads[1].wait()
    for kv in range(kvs):
        vt[kv, pl.ds(HEAD_DIM, 16), :] = jnp.ones((16, keys), BF16)

    def turn(c, carry):
        rows = pl.ds(pl.multiple_of(c * chunk, chunk), chunk)
        for kv in range(kvs):
            vt[kv, pl.ds(0, HEAD_DIM), rows] = vall[rows, kv * HEAD_DIM : (kv + 1) * HEAD_DIM].T
        return carry

    lax.fori_loop(0, keys // chunk, turn, 0)
    loads[2].wait()
    loads[3].wait()

    def q_wait(k, c):
        source = lax.rem(me + n - k, n)
        q_copy(k, source).wait_recv()
        return c

    lax.fori_loop(1, n, q_wait, 0)

    scale = HEAD_DIM ** (-0.5) * math.log2(math.e)

    def o_copy(dest, source):
        return to_seq(
            osend.at[dest], obuf.at[source], o_send.at[dest], o_recv.at[source], dest
        ), to_seq(ssend.at[dest], sbuf.at[source], s_send.at[dest], s_recv.at[source], dest)

    def attend(it, carry):
        kv, rb = it // blocks, it % blocks
        qs = qbuf[pl.ds(rb * BLOCK_REQS, BLOCK_REQS), kv].reshape(brows, HEAD_DIM)
        hot_row = lax.broadcasted_iota(jnp.int32, (brows, TILE), 0)
        hot_lane = lax.broadcasted_iota(jnp.int32, (brows, TILE), 1)
        hot = (hot_lane == rb * BLOCK_REQS + hot_row // ROWS) | (
            hot_lane == reqs + hot_row % NEW
        )
        q_aug = jnp.concatenate([qs, jnp.where(hot, 1.0, 0.0).astype(BF16)], axis=1)
        lanes = pl.ds(pl.multiple_of(kv * HEAD_DIM, HEAD_DIM), HEAD_DIM)

        def score(c, peak):
            rows = pl.ds(pl.multiple_of(c * chunk, chunk), chunk)
            k_aug = jnp.concatenate([kall[rows, lanes], mask[rows, :]], axis=1)
            s = lax.dot_general(
                k_aug, q_aug, (((1,), (1,)), ((), ())), preferred_element_type=F32
            )
            s_scr[rows, :] = s
            return jnp.maximum(peak, jnp.max(s.reshape(chunk // 8, 8, brows), axis=0))

        peak = lax.fori_loop(0, keys // chunk, score, jnp.full((8, brows), 4 * NEG, F32))
        peak = jnp.max(peak, axis=0, keepdims=True) * scale

        def weigh(c, acc):
            rows = pl.ds(pl.multiple_of(c * chunk, chunk), chunk)
            w = jnp.exp2(s_scr[rows, :] * scale - peak).astype(BF16)
            return acc + jnp.dot(vt[kv, :, rows], w, preferred_element_type=F32)

        acc = lax.fori_loop(
            0, keys // chunk, weigh, jnp.zeros((HEAD_DIM + 16, brows), F32)
        )
        row8 = lax.broadcasted_iota(jnp.int32, (8, brows), 0)
        stats = jnp.where(row8 == 0, peak, acc[HEAD_DIM : HEAD_DIM + 8])
        for i in range(per_block):
            dest = it * per_block + i
            cols = slice(i * TILE, (i + 1) * TILE)
            osend[dest] = acc[:HEAD_DIM, cols].astype(BF16)
            ssend[dest] = stats[:, cols]

            @pl.when(dest != me)
            def _():
                for copy in o_copy(dest, me):
                    copy.start()

        return carry

    lax.fori_loop(0, kvs * blocks, attend, 0)

    def a_place(source):
        return abuf.at[source // per_kv, pl.ds((source % per_kv) * CHUNK_REQS * NEW, CHUNK_REQS * NEW)]

    def a_copy(k, source):
        return to_seq(
            asend, a_place(source), a_send.at[k], a_recv.at[source], lax.rem(me + k, n)
        )

    def combine():
        obuf[me] = osend[me]
        sbuf[me] = ssend[me]

        def o_wait(k, c):
            source = lax.rem(me + n - k, n)
            for copy in o_copy(me, source):
                copy.wait_recv()
            return c

        lax.fori_loop(1, n, o_wait, 0)
        stats = sbuf[...]
        peak = stats[:, 0, :]
        factor = jnp.exp2(peak - jnp.max(peak, axis=0, keepdims=True))
        total = jnp.sum(stats[:, 1, :] * factor, axis=0, keepdims=True)
        outs = jnp.zeros((HEAD_DIM, TILE), F32)
        for source in range(n):
            outs = outs + obuf[source].astype(F32) * factor[source : source + 1]
        first = (me % per_kv) * CHUNK_REQS
        real = jnp.zeros((1, TILE), jnp.int32)
        for r in range(CHUNK_REQS):
            for j in range(NEW):
                real = jnp.where(
                    (lane // ROWS == r) & (lane % NEW == j), valid_ref[first + r, j], real
                )
        x = (outs / total * real.astype(F32)).astype(BF16)
        a = lax.broadcasted_iota(jnp.int32, (TILE, TILE), 0)
        b = lax.broadcasted_iota(jnp.int32, (TILE, TILE), 1)
        pick = b == ((a // NEW) % CHUNK_REQS) * ROWS + (a // (CHUNK_REQS * NEW)) * NEW + a % NEW
        y = lax.dot_general(
            jnp.where(pick, 1.0, 0.0).astype(BF16),
            x,
            (((1,), (1,)), ((), ())),
            preferred_element_type=F32,
        ).astype(BF16)
        step = CHUNK_REQS * NEW
        for h in range(HPK):
            asend[:, h * HEAD_DIM : (h + 1) * HEAD_DIM] = y[h * step : (h + 1) * step]
        abuf[me // per_kv, pl.ds((me % per_kv) * step, step), :] = asend[...]

        def a_start(k, c):
            a_copy(k, me).start()
            return c

        lax.fori_loop(1, n, a_start, 0)

    if all_combine:
        combine()
    else:
        pl.when(me < combiners)(combine)

    loads[4].wait()

    def a_wait(source, c):
        @pl.when(source != me)
        def _():
            a_copy(0, source).wait_recv()

        return c

    lax.fori_loop(0, combiners, a_wait, 0)
    width = HPK * HEAD_DIM
    terms = jnp.dot(abuf[0], wall[pl.ds(0, width), :], preferred_element_type=F32)
    for kv in range(1, kvs):
        terms = terms + jnp.dot(
            abuf[kv], wall[pl.ds(kv * width, width), :], preferred_element_type=F32
        )
    rows_out = out_ref.shape[0]
    tsend[...] = terms.reshape(tp, rows_out, terms.shape[1])

    def t_copy(k, peer, source):
        return pltpu.make_async_remote_copy(
            src_ref=tbuf.at[tp + k - 1],
            dst_ref=tbuf.at[source],
            send_sem=t_send.at[k],
            recv_sem=t_recv.at[source],
            device_id={"tp": peer},
            device_id_type=MESH,
        )

    for k in range(1, tp):
        peer = lax.rem(core + k, tp)
        tbuf[tp + k - 1] = tsend[peer].astype(BF16)
        t_copy(k, peer, core).start()
    out = tsend[core]
    for k in range(1, tp):
        source = lax.rem(core + tp - k, tp)
        t_copy(k, source, source).wait_recv()
        out = out + tbuf[source].astype(F32)
    out_ref[...] = out.astype(BF16)

    def q_done(k, c):
        q_copy(k, me).wait_send()
        return c

    lax.fori_loop(1, n, q_done, 0)

    def o_done(dest, c):
        @pl.when(dest != me)
        def _():
            for copy in o_copy(dest, me):
                copy.wait_send()

        return c

    lax.fori_loop(0, combiners, o_done, 0)

    def a_done():
        def one(k, c):
            a_copy(k, me).wait_send()
            return c

        lax.fori_loop(1, n, one, 0)

    if all_combine:
        a_done()
    else:
        pl.when(me < combiners)(a_done)
    for k in range(1, tp):
        t_copy(k, lax.rem(core + k, tp), core).wait_send()


def local(
    n,
    tp,
    queries,
    new_keys,
    new_values,
    prefix_keys,
    prefix_values,
    page_keys,
    page_values,
    out_weight,
    group_of,
    prefix_len,
    total_len,
    page_owner,
    page_slot,
    new_valid,
):
    reqs = group_of.shape[0]
    kvs = new_keys.shape[2] // HEAD_DIM
    pre = prefix_keys.shape[1]
    pages, page = page_keys.shape[:2]
    width = kvs * HEAD_DIM
    keys = GROUPS * pre + pages * page + TILE
    features = out_weight.shape[1]
    combiners = kvs * reqs // CHUNK_REQS
    rows_out = reqs * NEW // tp
    smem = pl.BlockSpec(memory_space=pltpu.SMEM)
    vmem = pl.BlockSpec(memory_space=pltpu.VMEM)
    hbm = pl.BlockSpec(memory_space=pl.ANY)
    dma = pltpu.SemaphoreType.DMA
    return pl.pallas_call(
        functools.partial(kernel, (n, tp, reqs, kvs, pre, pages, page)),
        out_shape=jax.ShapeDtypeStruct((rows_out, features), BF16),
        in_specs=[smem] * 6 + [vmem] * 3 + [hbm] * 5,
        out_specs=vmem,
        scratch_shapes=[
            pltpu.VMEM((keys, width), BF16),
            pltpu.VMEM((keys, width), BF16),
            pltpu.VMEM(out_weight.shape, BF16),
            pltpu.VMEM((kvs, HEAD_DIM + 16, keys), BF16),
            pltpu.VMEM((keys, TILE), BF16),
            pltpu.VMEM((16, width), F32),
            pltpu.VMEM((kvs * ROWS, HEAD_DIM), F32),
            pltpu.VMEM((reqs, kvs, ROWS, HEAD_DIM), BF16),
            pltpu.VMEM((keys, BLOCK_REQS * ROWS), F32),
            pltpu.VMEM((combiners, HEAD_DIM, TILE), BF16),
            pltpu.VMEM((combiners, 8, TILE), F32),
            pltpu.VMEM((n, HEAD_DIM, TILE), BF16),
            pltpu.VMEM((n, 8, TILE), F32),
            pltpu.VMEM((CHUNK_REQS * NEW, HPK * HEAD_DIM), BF16),
            pltpu.VMEM((kvs, reqs * NEW, HPK * HEAD_DIM), BF16),
            pltpu.VMEM((tp, rows_out, features), F32),
            pltpu.VMEM((2 * tp - 1, rows_out, features), BF16),
            dma((5,)),
            dma((n,)),
            dma((n,)),
            dma((combiners,)),
            dma((n,)),
            dma((combiners,)),
            dma((n,)),
            dma((n,)),
            dma((n,)),
            dma((tp,)),
            dma((tp,)),
        ],
        compiler_params=pltpu.CompilerParams(
            collective_id=0, has_side_effects=True, vmem_limit_bytes=48 * 2**20
        ),
    )(
        group_of,
        prefix_len,
        total_len,
        page_owner,
        page_slot,
        new_valid,
        queries,
        new_keys,
        new_values,
        prefix_keys.reshape(GROUPS * pre, width),
        prefix_values.reshape(GROUPS * pre, width),
        page_keys.reshape(pages * page, width),
        page_values.reshape(pages * page, width),
        out_weight,
    )


def solution(mesh):
    placed = (
        P("seq", None, "tp"),
        P("seq", None, "tp"),
        P("seq", None, "tp"),
        P(None, "seq", "tp"),
        P(None, "seq", "tp"),
        P("seq", None, "tp"),
        P("seq", None, "tp"),
        P("tp", "seq"),
        P(),
        P(),
        P(),
        P("seq"),
        P("seq"),
        P(),
    )
    return jax.shard_map(
        functools.partial(local, mesh.shape["seq"], mesh.shape["tp"]),
        mesh=mesh,
        in_specs=placed,
        out_specs=P("tp", "seq"),
        check_vma=False,
    )
```

time: 426 us -> 76.8 us (0.18)
  the two profiles are of different devices: /device:TPU:1 before, /device:TPU:21 now
where the time goes in v1:
time: 76.8 us; the launch traced here: 76.4 us
  Pallas kernels  64.3 us (84%)
  local copies, waits for them, and re-layouts  12 us (16%)
    pallas_call x1, Pallas kernels, local(): pl.pallas_call(functools.partial(kernel, (n, tp, reqs, kvs, pre, pages, p...  64.3 us
    unnamed x26, local copies, waits for them, and re-layouts  12 us

profile of v1, /device:TPU:21, one launch (start us, length us, event | category | flops | bytes accessed | tf_op | source)
XLA Modules:
  0.0 76.4 jit_solution(9711801360394232371)
XLA Ops:
  0.0 0.8 copy.15.valid_ref
  0.8 0.0 copy-start
  0.8 1.4 %copy-done = bf16[8,192,512]{2,1,0:T(8,128)(2,1)S(1)} copy-done((bf16[8,192,512]{2,1,0:T(8,128)(2,1)S(1)}, bf16[8,192,512]{2,1,0:T(8,128)(2,1)}, u32[]{:S(2)}) %copy-start) | copy-done | bytes 1572888
  2.2 0.0 copy-start.1
  2.2 1.4 %copy-done.1 = bf16[8,192,512]{2,1,0:T(8,128)(2,1)S(1)} copy-done((bf16[8,192,512]{2,1,0:T(8,128)(2,1)S(1)}, bf16[8,192,512]{2,1,0:T(8,128)(2,1)}, u32[]{:S(2)}) %copy-start.1) | copy-done | bytes 1572888
  3.6 0.0 copy-start.2
  3.6 1.2 %copy-done.2 = bf16[16,64,512]{2,1,0:T(8,128)(2,1)S(1)} copy-done((bf16[16,64,512]{2,1,0:T(8,128)(2,1)S(1)}, bf16[16,64,512]{2,1,0:T(8,128)(2,1)}, u32[]{:S(2)}) %copy-start.2) | copy-done | bytes 1048600
  4.8 0.0 copy-start.3
  4.8 1.2 %copy-done.3 = bf16[16,64,512]{2,1,0:T(8,128)(2,1)S(1)} copy-done((bf16[16,64,512]{2,1,0:T(8,128)(2,1)S(1)}, bf16[16,64,512]{2,1,0:T(8,128)(2,1)}, u32[]{:S(2)}) %copy-start.3) | copy-done | bytes 1048600
  6.0 0.0 copy-start.4
  6.0 0.8 copy-done.4
  6.8 0.0 copy-start.5
  6.8 0.7 copy-done.5
  7.5 0.0 copy-start.6
  7.5 0.7 copy-done.6
  8.2 0.0 copy-start.7
  8.2 0.7 copy-done.7
  8.8 0.0 copy-start.8
  8.8 0.7 copy-done.8
  9.5 0.0 copy-start.9
  9.5 0.7 copy-done.9
  10.1 0.0 copy-start.10
  10.1 0.7 copy-done.10
  10.8 0.0 copy-start.11
  10.8 0.7 copy-done.11
  11.4 64.3 %shard_map.136 = bf16[32,512]{1,0:T(8,128)(2,1)S(1)} custom-call(s32[16]{0:T(128)S(1)} %copy-done.7, s32[8]{0:T(128)S(1)} %copy-done.8, s32[16]{0:T(128)S(1)} %copy-done.9, s32[16]{0:T(128)S(1)} %copy-done.10, s32[16]{0:T(128)S(1)} %copy-done.11, s32[16,4]{1,0:T(8,128)S(1)} %copy.15.valid_ref, bf16[1,4,4096]{2,1,0:T(4,128)(2,1)S(1)} %copy-done.4, ...), custom_call_target="tpu_custom_call" | custom-call | tf_op jit(solution)/shard_map/pallas_call | solution.py:420
  75.7 0.6 copy.17
Async XLA Ops:
  0.8 1.4 %copy-start = (bf16[8,192,512]{2,1,0:T(8,128)(2,1)S(1)}, bf16[8,192,512]{2,1,0:T(8,128)(2,1)}, u32[]{:S(2)}) copy-start(bf16[8,192,512]{2,1,0:T(8,128)(2,1)} %param.17) | copy-start | bytes 4718596
  2.2 1.4 %copy-start.1 = (bf16[8,192,512]{2,1,0:T(8,128)(2,1)S(1)}, bf16[8,192,512]{2,1,0:T(8,128)(2,1)}, u32[]{:S(2)}) copy-start(bf16[8,192,512]{2,1,0:T(8,128)(2,1)} %param.18) | copy-start | bytes 4718596
  3.6 1.2 %copy-start.2 = (bf16[16,64,512]{2,1,0:T(8,128)(2,1)S(1)}, bf16[16,64,512]{2,1,0:T(8,128)(2,1)}, u32[]{:S(2)}) copy-start(bf16[16,64,512]{2,1,0:T(8,128)(2,1)} %param.19) | copy-start | bytes 3145732
  4.8 1.2 %copy-start.3 = (bf16[16,64,512]{2,1,0:T(8,128)(2,1)S(1)}, bf16[16,64,512]{2,1,0:T(8,128)(2,1)}, u32[]{:S(2)}) copy-start(bf16[16,64,512]{2,1,0:T(8,128)(2,1)} %param.20) | copy-start | bytes 3145732
  6.0 0.8 copy-start.4
  6.8 0.7 copy-start.5
  7.5 0.7 copy-start.6
  8.2 0.7 copy-start.7
  8.8 0.7 copy-start.8
  9.5 0.7 copy-start.9
  10.1 0.7 copy-start.10
  10.8 0.7 copy-start.11

commit v2 on v1

--- a/solution.py
+++ b/solution.py
@@ -16,6 +16,7 @@
 BLOCK_REQS = 16
 CHUNK_REQS = 4
 TILE = 128
+PLANE = 4
 NEG = -1e30
 MESH = pl.DeviceIdType.MESH
 F32 = jnp.float32
@@ -52,7 +53,6 @@
     ssend,
     obuf,
     sbuf,
-    asend,
     abuf,
     tsend,
     tbuf,
@@ -128,16 +128,67 @@
             device_id_type=MESH,
         )
 
-    def q_copy(k, source):
-        return to_seq(
-            qbuf.at[source], qbuf.at[source], q_send.at[k], q_recv.at[source], lax.rem(me + k, n)
-        )
-
-    def q_start(k, c):
-        q_copy(k, me).start()
-        return c
-
-    lax.fori_loop(1, n, q_start, 0)
+    base, place_in = me // PLANE * PLANE, me % PLANE
+    layers = n // PLANE
+
+    def spread(place, send, recv, sources):
+        def copy(source, peer, k):
+            return to_seq(place(source), place(source), send.at[k], recv.at[source], peer)
+
+        def along(k):
+            return copy(me, lax.rem(me + k * PLANE, n), k)
+
+        def within(k, source, p):
+            return copy(
+                source, base + lax.rem(place_in + p, PLANE), layers + k * (PLANE - 1) + p - 1
+            )
+
+        def held(source, act):
+            if sources == n:
+                act()
+            else:
+                pl.when(source < sources)(act)
+
+        def above(k):
+            return lax.rem(me + n - k * PLANE, n)
+
+        def start():
+            for k in range(1, layers):
+                along(k).start()
+            for p in range(1, PLANE):
+                within(0, me, p).start()
+
+        def relay():
+            for k in range(1, layers):
+                source = above(k)
+
+                def pass_on():
+                    copy(source, me, 0).wait_recv()
+                    for p in range(1, PLANE):
+                        within(k, source, p).start()
+
+                held(source, pass_on)
+
+        def finish():
+            for p in range(1, PLANE):
+                for k in range(layers):
+                    source = lax.rem(base + lax.rem(place_in + p, PLANE) + n - k * PLANE, n)
+                    held(source, lambda: copy(source, me, 0).wait_recv())
+
+        def done():
+            def own():
+                for k in range(1, layers):
+                    along(k).wait_send()
+
+            held(me, own)
+            for k in range(layers):
+                for p in range(1, PLANE):
+                    held(above(k), lambda: within(k, above(k), p).wait_send())
+
+        return start, relay, finish, done
+
+    q_start, q_relay, q_finish, q_done = spread(lambda source: qbuf.at[source], q_send, q_recv, n)
+    q_start()
 
     lane = lax.broadcasted_iota(jnp.int32, (1, TILE), 1)
     group_vec = jnp.full((1, TILE), -1, jnp.int32)
@@ -165,7 +216,7 @@
     row_new = lax.broadcasted_iota(jnp.int32, (TILE, TILE), 0)
     valid_rows = jnp.zeros((TILE, TILE), jnp.int32)
     for i in range(NEW):
-        valid_rows = jnp.where(row_new == i, valid_ref[me, i], valid_rows)
+        valid_rows = jnp.where(row_new == i, valid_ref[i, me], valid_rows)
     alive = (
         (valid_rows == 1)
         & ((lane_new == me) | ((lane_new >= reqs) & (row_new <= lane_new - reqs)))
@@ -173,6 +224,8 @@
     )
     mask[pl.ds(cached, TILE), :] = jnp.where(alive, 0.0, NEG).astype(BF16)
 
+    q_relay()
+
     for new_ref, all_ref in ((nk_ref, kall), (nv_ref, vall)):
         tmp[...] = jnp.zeros_like(tmp)
         tmp[pl.ds(0, NEW), :] = new_ref[0].astype(F32)
@@ -194,12 +247,7 @@
     loads[2].wait()
     loads[3].wait()
 
-    def q_wait(k, c):
-        source = lax.rem(me + n - k, n)
-        q_copy(k, source).wait_recv()
-        return c
-
-    lax.fori_loop(1, n, q_wait, 0)
+    q_finish()
 
     scale = HEAD_DIM ** (-0.5) * math.log2(math.e)
 
@@ -208,7 +256,8 @@
             osend.at[dest], obuf.at[source], o_send.at[dest], o_recv.at[source], dest
         ), to_seq(ssend.at[dest], sbuf.at[source], s_send.at[dest], s_recv.at[source], dest)
 
-    def attend(it, carry):
+    def attend(turn_idx, carry):
+        it = lax.rem(turn_idx + 1 + me // PLANE, kvs * blocks)
         kv, rb = it // blocks, it % blocks
         qs = qbuf[pl.ds(rb * BLOCK_REQS, BLOCK_REQS), kv].reshape(brows, HEAD_DIM)
         hot_row = lax.broadcasted_iota(jnp.int32, (brows, TILE), 0)
@@ -259,10 +308,7 @@
     def a_place(source):
         return abuf.at[source // per_kv, pl.ds((source % per_kv) * CHUNK_REQS * NEW, CHUNK_REQS * NEW)]
 
-    def a_copy(k, source):
-        return to_seq(
-            asend, a_place(source), a_send.at[k], a_recv.at[source], lax.rem(me + k, n)
-        )
+    a_start, a_relay, a_finish, a_done = spread(a_place, a_send, a_recv, combiners)
 
     def combine():
         obuf[me] = osend[me]
@@ -287,7 +333,7 @@
         for r in range(CHUNK_REQS):
             for j in range(NEW):
                 real = jnp.where(
-                    (lane // ROWS == r) & (lane % NEW == j), valid_ref[first + r, j], real
+                    (lane // ROWS == r) & (lane % NEW == j), valid_ref[j, first + r], real
                 )
         x = (outs / total * real.astype(F32)).astype(BF16)
         a = lax.broadcasted_iota(jnp.int32, (TILE, TILE), 0)
@@ -300,31 +346,21 @@
             preferred_element_type=F32,
         ).astype(BF16)
         step = CHUNK_REQS * NEW
+        rows = pl.ds((me % per_kv) * step, step)
         for h in range(HPK):
-            asend[:, h * HEAD_DIM : (h + 1) * HEAD_DIM] = y[h * step : (h + 1) * step]
-        abuf[me // per_kv, pl.ds((me % per_kv) * step, step), :] = asend[...]
-
-        def a_start(k, c):
-            a_copy(k, me).start()
-            return c
-
-        lax.fori_loop(1, n, a_start, 0)
+            abuf[me // per_kv, rows, h * HEAD_DIM : (h + 1) * HEAD_DIM] = y[
+                h * step : (h + 1) * step
+            ]
+        a_start()
 
     if all_combine:
         combine()
     else:
         pl.when(me < combiners)(combine)
 
+    a_relay()
     loads[4].wait()
-
-    def a_wait(source, c):
-        @pl.when(source != me)
-        def _():
-            a_copy(0, source).wait_recv()
-
-        return c
-
-    lax.fori_loop(0, combiners, a_wait, 0)
+    a_finish()
     width = HPK * HEAD_DIM
     terms = jnp.dot(abuf[0], wall[pl.ds(0, width), :], preferred_element_type=F32)
     for kv in range(1, kvs):
@@ -355,11 +391,7 @@
         out = out + tbuf[source].astype(F32)
     out_ref[...] = out.astype(BF16)
 
-    def q_done(k, c):
-        q_copy(k, me).wait_send()
-        return c
-
-    lax.fori_loop(1, n, q_done, 0)
+    q_done()
 
     def o_done(dest, c):
         @pl.when(dest != me)
@@ -371,17 +403,7 @@
 
     lax.fori_loop(0, combiners, o_done, 0)
 
-    def a_done():
-        def one(k, c):
-            a_copy(k, me).wait_send()
-            return c
-
-        lax.fori_loop(1, n, one, 0)
-
-    if all_combine:
-        a_done()
-    else:
-        pl.when(me < combiners)(a_done)
+    a_done()
     for k in range(1, tp):
         t_copy(k, lax.rem(core + k, tp), core).wait_send()
 
@@ -415,7 +437,7 @@
     rows_out = reqs * NEW // tp
     smem = pl.BlockSpec(memory_space=pltpu.SMEM)
     vmem = pl.BlockSpec(memory_space=pltpu.VMEM)
-    hbm = pl.BlockSpec(memory_space=pl.ANY)
+    hbm = pl.BlockSpec(memory_space=pltpu.HBM)
     dma = pltpu.SemaphoreType.DMA
     return pl.pallas_call(
         functools.partial(kernel, (n, tp, reqs, kvs, pre, pages, page)),
@@ -436,7 +458,6 @@
             pltpu.VMEM((combiners, 8, TILE), F32),
             pltpu.VMEM((n, HEAD_DIM, TILE), BF16),
             pltpu.VMEM((n, 8, TILE), F32),
-            pltpu.VMEM((CHUNK_REQS * NEW, HPK * HEAD_DIM), BF16),
             pltpu.VMEM((kvs, reqs * NEW, HPK * HEAD_DIM), BF16),
             pltpu.VMEM((tp, rows_out, features), F32),
             pltpu.VMEM((2 * tp - 1, rows_out, features), BF16),
@@ -453,7 +474,7 @@
             dma((tp,)),
         ],
         compiler_params=pltpu.CompilerParams(
-            collective_id=0, has_side_effects=True, vmem_limit_bytes=48 * 2**20
+            collective_id=0, has_side_effects=True, vmem_limit_bytes=63 * 2**20
         ),
     )(
         group_of,
@@ -461,7 +482,7 @@
         total_len,
         page_owner,
         page_slot,
-        new_valid,
+        new_valid.T,
         queries,
         new_keys,
         new_values,

time: 76.8 us -> 52.5 us (0.68)
  the two profiles are of different devices: /device:TPU:21 before, /device:TPU:1 now
where the time goes in v2:
time: 52.5 us; the launch traced here: 52.2 us
  Pallas kernels  50.8 us (97%)
  local copies, waits for them, and re-layouts  1.38 us (3%)
    pallas_call x1, Pallas kernels, local(): pl.pallas_call(functools.partial(kernel, (n, tp, reqs, kvs, pre, pages, p...  50.8 us
    unnamed x1, local copies, waits for them, and re-layouts  1.38 us

profile of v2, /device:TPU:1, one launch (start us, length us, event | category | flops | bytes accessed | tf_op | source)
XLA Modules:
  0.0 52.2 jit_solution(11385813714332554455)
XLA Ops:
  0.0 50.8 %shard_map.136 = bf16[32,512]{1,0:T(8,128)(2,1)} custom-call(s32[16]{0:T(128)} %group_ref.1, s32[8]{0:T(128)} %plen_ref.1, s32[16]{0:T(128)} %tlen_ref.1, s32[16]{0:T(128)} %owner_ref.1, s32[16]{0:T(128)} %slot_ref.1, s32[4,16]{1,0:T(4,128)} %bitcast.9, bf16[1,4,4096]{2,1,0:T(4,128)(2,1)} %q_ref.1, bf16[1,4,512]{2,1,0:T(4,128)(2,1)} %nk_ref.1, ...), custom_call_target="tpu_custom_call" | custom-call | tf_op jit(solution)/shard_map/pallas_call | solution.py:442
  50.8 1.4 %copy.16 = bf16[32,512]{1,0:T(8,128)(2,1)} copy(bf16[32,512]{1,0:T(8,128)(2,1)} %shard_map.136) | data formatting | bytes 65536

commit v3 on v2

--- a/solution.py
+++ b/solution.py
@@ -72,7 +72,7 @@
     pre_rows, page_rows = GROUPS * pre, pages * page
     cached = pre_rows + page_rows
     keys = cached + TILE
-    chunk = 384 if keys % 384 == 0 else TILE
+    chunk = 896 if keys % 896 == 0 else TILE
     blocks = reqs // BLOCK_REQS
     brows = BLOCK_REQS * ROWS
     per_kv = reqs // CHUNK_REQS
@@ -277,7 +277,7 @@
             s_scr[rows, :] = s
             return jnp.maximum(peak, jnp.max(s.reshape(chunk // 8, 8, brows), axis=0))
 
-        peak = lax.fori_loop(0, keys // chunk, score, jnp.full((8, brows), 4 * NEG, F32))
+        peak = lax.fori_loop(0, keys // chunk, score, jnp.full((8, brows), 4 * NEG, F32), unroll=True)
         peak = jnp.max(peak, axis=0, keepdims=True) * scale
 
         def weigh(c, acc):
@@ -286,7 +286,7 @@
             return acc + jnp.dot(vt[kv, :, rows], w, preferred_element_type=F32)
 
         acc = lax.fori_loop(
-            0, keys // chunk, weigh, jnp.zeros((HEAD_DIM + 16, brows), F32)
+            0, keys // chunk, weigh, jnp.zeros((HEAD_DIM + 16, brows), F32), unroll=True
         )
         row8 = lax.broadcasted_iota(jnp.int32, (8, brows), 0)
         stats = jnp.where(row8 == 0, peak, acc[HEAD_DIM : HEAD_DIM + 8])

time: 52.5 us -> 47.8 us (0.910)
  Pallas kernels: 50.8 us -> 46.1 us
    pallas_call x1, Pallas kernels: 50.8 us -> 46.1 us  [local(): pl.pallas_call(functools.partial(kernel, (n, tp, reqs, kvs, pre, pages, p...]
where the time goes in v3:
time: 47.8 us; the launch traced here: 47.5 us
  Pallas kernels  46.1 us (96%)
  local copies, waits for them, and re-layouts  1.38 us (3%)
    pallas_call x1, Pallas kernels, local(): pl.pallas_call(functools.partial(kernel, (n, tp, reqs, kvs, pre, pages, p...  46.1 us
    unnamed x1, local copies, waits for them, and re-layouts  1.38 us

profile of v3, /device:TPU:1, one launch (start us, length us, event | category | flops | bytes accessed | tf_op | source)
XLA Modules:
  0.0 47.5 jit_solution(6625632946891595446)
XLA Ops:
  0.0 46.1 %shard_map.136 = bf16[32,512]{1,0:T(8,128)(2,1)} custom-call(s32[16]{0:T(128)} %group_ref.1, s32[8]{0:T(128)} %plen_ref.1, s32[16]{0:T(128)} %tlen_ref.1, s32[16]{0:T(128)} %owner_ref.1, s32[16]{0:T(128)} %slot_ref.1, s32[4,16]{1,0:T(4,128)} %bitcast.9, bf16[1,4,4096]{2,1,0:T(4,128)(2,1)} %q_ref.1, bf16[1,4,512]{2,1,0:T(4,128)(2,1)} %nk_ref.1, ...), custom_call_target="tpu_custom_call" | custom-call | tf_op jit(solution)/shard_map/pallas_call | solution.py:442
  46.2 1.4 %copy.16 = bf16[32,512]{1,0:T(8,128)(2,1)} copy(bf16[32,512]{1,0:T(8,128)(2,1)} %shard_map.136) | data formatting | bytes 65536
